TPU v7x, 32 devices: a whole 2x2x4 slice. The times are simulated.
32 devices in a mesh: dp: 16 (over z, x, core), tensor: 2 (over y).
Axes of the slice: x: 2, y: 2, z: 4, core: 2. Of those that a mesh axis runs over, the one named last changes fastest.
Arguments:
- x_hidden: bfloat16 [4096, 8192], P('dp', 'tensor'), may hold values from -6 to 6
- norm_gain: bfloat16 [8192], P('tensor'), may hold values from 0.25 to 1.75
- queries_upper: bfloat16 [4096, 4096], P('dp', 'tensor'), may hold values from -6 to 6
- block_key_value_above: bfloat16 [2, 4096, 1024], P(None, 'dp', 'tensor'), may hold values from -6 to 6
- out_grad_upper: bfloat16 [4096, 4096], P('dp', 'tensor'), may hold values from -6 to 6
- resid_grad: bfloat16 [4096, 8192], P('dp', 'tensor'), may hold values from -2 to 2
- queries_lower: bfloat16 [4096, 4096], P('dp', 'tensor'), may hold values from -6 to 6
- block_key_value_below: bfloat16 [2, 4096, 1024], P(None, 'dp', 'tensor'), may hold values from -6 to 6
- w_query: bfloat16 [8192, 4096], P('dp', 'tensor'), may hold values from -0.0625 to 0.0625
- key_weight_above: bfloat16 [8192, 1024], P('dp', 'tensor'), may hold values from -0.0625 to 0.0625
- value_weight_above: bfloat16 [8192, 1024], P('dp', 'tensor'), may hold values from -0.0625 to 0.0625
- w_output: bfloat16 [4096, 8192], P('tensor', 'dp'), may hold values from -0.09375 to 0.09375
- prefix_upper: bfloat16 [2, 2048, 1024], P(None, None, 'tensor'), may hold values from -6 to 6
- prefix_lower: bfloat16 [2, 2048, 1024], P(None, None, 'tensor'), may hold values from -6 to 6
- master: float32 [2, 2, 2048, 1024], P(None, None, 'dp', 'tensor'), may hold values from -6 to 6
- first_moment_state: float32 [2, 2, 2048, 1024], P(None, None, 'dp', 'tensor'), may hold values from -0.046875 to 0.046875
- second_moment_state: float32 [2, 2, 2048, 1024], P(None, None, 'dp', 'tensor'), may hold values from 0.0001 to 0.01
- offsets: int32 [16], P('dp'), may hold values from 0 to 2047
Outputs:
- new_master: float32 [2, 2, 2048, 1024], P(None, None, 'dp', 'tensor')
- new_moment_one: float32 [2, 2, 2048, 1024], P(None, None, 'dp', 'tensor')
- new_moment_two: float32 [2, 2, 2048, 1024], P(None, None, 'dp', 'tensor')
All inputs are finite; a program needn't handle non-finite values.
Results may differ from a plain program's by a relative error of at most 0.0052.
The roundings to bfloat16 on the way count: a program that leaves them out, or rounds other values in their place, can miss the bound.
Values may be sent and summed in bfloat16 or wider, within the bound.
A program may use at most 320 MiB of HBM per device.

v0:
```python
import jax
import jax.numpy as jnp
from jax import lax
from jax.sharding import PartitionSpec as P

MODEL_WIDTH = 8192
HEAD_SIZE = 128
PREFIX_SLOTS = 2048


norm_eps = 1e-05
rope_base = 500000.0
adam_rate = 0.05
beta_one = 0.9
beta_two = 0.999
adam_count = 10.0
adam_eps = 1e-08


def attend_back(queries, keys, values, out_grad):
    rows = queries.shape[0]
    key_rows = keys.shape[0]
    kv_heads = keys.shape[1] // HEAD_SIZE
    group = queries.shape[1] // HEAD_SIZE // kv_heads
    scale = HEAD_SIZE ** (-0.5)
    query_h = queries.reshape(rows, kv_heads, group, HEAD_SIZE)
    key_h = keys.reshape(key_rows, kv_heads, HEAD_SIZE)
    value_h = values.reshape(key_rows, kv_heads, HEAD_SIZE)
    grad_h = out_grad.reshape(rows, kv_heads, group, HEAD_SIZE)
    scores = (
        jnp.einsum("tkgd,ukd->kgtu", query_h, key_h, preferred_element_type=jnp.float32) * scale
    )
    row_ids = jnp.arange(rows)[:, None]
    col_ids = jnp.arange(key_rows)[None, :]
    allowed = (col_ids < PREFIX_SLOTS) | (col_ids - PREFIX_SLOTS <= row_ids)
    scores = jnp.where(allowed, scores, -jnp.inf)
    top = jnp.max(scores, axis=-1, keepdims=True)
    expo = jnp.exp(scores - top)
    probs = expo / jnp.sum(expo, axis=-1, keepdims=True)
    probs_b = probs.astype(jnp.bfloat16)
    attn = jnp.einsum("kgtu,ukd->tkgd", probs_b, value_h, preferred_element_type=jnp.float32)
    delta = jnp.transpose(jnp.sum(grad_h.astype(jnp.float32) * attn, axis=-1), (1, 2, 0))
    dprob = jnp.einsum("tkgd,ukd->kgtu", grad_h, value_h, preferred_element_type=jnp.float32)
    dscore = (probs * (dprob - delta[..., None])).astype(jnp.bfloat16)
    grad_query = (
        jnp.einsum("kgtu,ukd->tkgd", dscore, key_h, preferred_element_type=jnp.float32) * scale
    )
    grad_key = (
        jnp.einsum("kgtu,tkgd->ukd", dscore, query_h, preferred_element_type=jnp.float32) * scale
    )
    grad_value = jnp.einsum("kgtu,tkgd->ukd", probs_b, grad_h, preferred_element_type=jnp.float32)
    return (
        grad_query.reshape(rows, -1),
        grad_key.reshape(key_rows, -1),
        grad_value.reshape(key_rows, -1),
    )


def rotate_back(grad, positions):
    half = HEAD_SIZE // 2
    shaped = grad.reshape(grad.shape[:-1] + (grad.shape[-1] // HEAD_SIZE, HEAD_SIZE))
    freqs = jnp.exp(-jnp.log(rope_base) * 2.0 * jnp.arange(half).astype(jnp.float32) / HEAD_SIZE)
    angle = positions[..., None, None] * freqs
    cosine = jnp.cos(angle)
    sine = jnp.sin(angle)
    first = shaped[..., :half]
    second = shaped[..., half:]
    out_first = first * cosine + second * sine
    out_second = second * cosine - first * sine
    return jnp.concatenate([out_first, out_second], axis=-1).reshape(grad.shape)


def layer_back(queries, block_kv, prefix, out_grad):
    keys = jnp.concatenate([prefix[0], block_kv[0]], axis=0)
    values = jnp.concatenate([prefix[1], block_kv[1]], axis=0)
    return attend_back(queries, keys, values, out_grad)


def per_device(
    x_hidden,
    norm_gain,
    queries_upper,
    block_key_value_above,
    out_grad_upper,
    resid_grad,
    queries_lower,
    block_key_value_below,
    w_query,
    key_weight_above,
    value_weight_above,
    w_output,
    prefix_upper,
    prefix_lower,
    master,
    first_moment_state,
    second_moment_state,
    offsets,
):
    tokens = queries_upper.shape[0]
    grad_query, grad_key, grad_value = layer_back(
        queries_upper, block_key_value_above, prefix_upper, out_grad_upper
    )
    positions = (PREFIX_SLOTS + offsets[0] + jnp.arange(tokens)).astype(jnp.float32)
    query_rot = rotate_back(grad_query, positions).astype(jnp.bfloat16)
    key_rot = rotate_back(grad_key[PREFIX_SLOTS:], positions).astype(jnp.bfloat16)
    value_rot = grad_value[PREFIX_SLOTS:].astype(jnp.bfloat16)
    columns = jnp.einsum(
        "tc,nc->tn",
        query_rot,
        lax.all_gather(w_query, "dp", axis=0, tiled=True),
        preferred_element_type=jnp.float32,
    )
    columns = columns + jnp.einsum(
        "tc,nc->tn",
        key_rot,
        lax.all_gather(key_weight_above, "dp", axis=0, tiled=True),
        preferred_element_type=jnp.float32,
    )
    columns = columns + jnp.einsum(
        "tc,nc->tn",
        value_rot,
        lax.all_gather(value_weight_above, "dp", axis=0, tiled=True),
        preferred_element_type=jnp.float32,
    )
    partial_grad = columns
    hidden_grad = lax.psum_scatter(partial_grad, "tensor", scatter_dimension=1, tiled=True)
    hidden_f = x_hidden.astype(jnp.float32)
    gained = norm_gain.astype(jnp.float32) * hidden_grad
    square_sum, cross_sum = lax.psum(
        (jnp.sum(hidden_f * hidden_f, axis=-1), jnp.sum(hidden_f * gained, axis=-1)), "tensor"
    )
    recip = 1.0 / jnp.sqrt(square_sum[:, None] / MODEL_WIDTH + norm_eps)
    cross = cross_sum[:, None] / MODEL_WIDTH
    grad_local = resid_grad.astype(jnp.float32) + recip * gained - hidden_f * recip**3 * cross
    grad_hidden = lax.all_gather(grad_local.astype(jnp.bfloat16), "tensor", axis=1, tiled=True)
    columns = grad_hidden
    out_grad_lower = jnp.einsum(
        "td,hd->th",
        columns,
        lax.all_gather(w_output, "dp", axis=1, tiled=True),
        preferred_element_type=jnp.float32,
    ).astype(jnp.bfloat16)
    lower_query, lower_key, lower_value = layer_back(
        queries_lower, block_key_value_below, prefix_lower, out_grad_lower
    )
    grads = jnp.stack(
        [
            jnp.stack([lower_key[:PREFIX_SLOTS], lower_value[:PREFIX_SLOTS]]),
            jnp.stack([grad_key[:PREFIX_SLOTS], grad_value[:PREFIX_SLOTS]]),
        ]
    )
    whole_grads = lax.psum(grads, "dp")
    share_rows = PREFIX_SLOTS // lax.axis_size("dp")
    own_grads = lax.dynamic_slice_in_dim(
        whole_grads, lax.axis_index("dp") * share_rows, share_rows, 2
    )
    new_moment_one = beta_one * first_moment_state + (1.0 - beta_one) * own_grads
    new_moment_two = beta_two * second_moment_state + (1.0 - beta_two) * own_grads * own_grads
    first_hat = new_moment_one / (1.0 - beta_one**adam_count)
    second_hat = new_moment_two / (1.0 - beta_two**adam_count)
    new_master = master - adam_rate * first_hat / (jnp.sqrt(second_hat) + adam_eps)
    return (new_master, new_moment_one, new_moment_two)


def solution(mesh):
    return jax.shard_map(
        per_device,
        mesh=mesh,
        in_specs=(
            P("dp", "tensor"),
            P("tensor"),
            P("dp", "tensor"),
            P(None, "dp", "tensor"),
            P("dp", "tensor"),
            P("dp", "tensor"),
            P("dp", "tensor"),
            P(None, "dp", "tensor"),
            P("dp", "tensor"),
            P("dp", "tensor"),
            P("dp", "tensor"),
            P("tensor", "dp"),
            P(None, None, "tensor"),
            P(None, None, "tensor"),
            P(None, None, "dp", "tensor"),
            P(None, None, "dp", "tensor"),
            P(None, None, "dp", "tensor"),
            P("dp"),
        ),
        out_specs=(
            P(None, None, "dp", "tensor"),
            P(None, None, "dp", "tensor"),
            P(None, None, "dp", "tensor"),
        ),
        check_vma=False,
    )
```

profile of v0, /device:TPU:0, one launch (start us, length us, event | category | flops | bytes accessed | tf_op | source)
XLA Modules:
  0.0 1066.3 jit_solution(16773761373981669107)
XLA Ops:
  24.0 19.7 %fusion.58 = (f32[4,4,256]{2,1,0:T(4,128)S(1)}, f32[4,4,256,2304]{2,3,1,0:T(8,128)}) fusion(bf16[256,4,4,128]{0,3,2,1:T(8,128)(2,1)} %bitcast.182, pred[256,2304]{0,1:T(8,128)(4,1)S(1)} %fusion.31, bf16[256,4,128]{2,0,1:T(8,128)(2,1)S(1)} %copy.120, bf16[2048,4,128]{2,0,1:T(8,128)(2,1)S(1)} %copy.119), kind=kOutput, calls=%fused_computation.99 | convolution fusion | flops 2458388736 | bytes 41762816 | tf_op jit(solution)/shard_map/sub | solution.py:38
  44.3 21.6 %fusion.19 = bf16[4,4,256,2304]{2,3,1,0:T(8,128)(2,1)} fusion(f32[4,4,256,2304]{2,3,1,0:T(8,128)} %get-tuple-element.27, f32[4,4,256]{2,1,0:T(4,128)S(1)} %get-tuple-element.26), kind=kLoop, calls=%fused_computation.26 | loop fusion | flops 18874368 | bytes 56639488 | tf_op jit(solution)/shard_map/convert_element_type | solution.py:40
  78.0 10.5 convolution_bitcast_fusion.1
  88.9 10.8 %fusion.33 = f32[256,4,4]{0,2,1:T(4,128)S(1)} fusion(bf16[256,4,4,128]{0,3,2,1:T(8,128)(2,1)S(1)} %bitcast.172, bf16[4,4,256,2304]{2,3,1,0:T(8,128)(2,1)} %fusion.19, bf16[256,4,128]{2,0,1:T(8,128)(2,1)S(1)} %copy-done.5, bf16[2048,4,128]{2,0,1:T(8,128)(2,1)S(1)} %copy-done.2), kind=kOutput, calls=%fused_computation.58 | convolution fusion | flops 2422206464 | bytes 22298624 | tf_op jit(solution)/shard_map/kgtu,ukd->tkgd/dot_general | solution.py:41
  99.7 20.5 %fusion.5 = bf16[4,4,256,2304]{2,3,1,0:T(8,128)(2,1)} fusion(bf16[256,4,4,128]{0,3,2,1:T(8,128)(2,1)S(1)} %bitcast.173, f32[4,4,256]{2,1,0:T(4,128)S(1)} %bitcast.194, f32[4,4,256,2304]{2,3,1,0:T(8,128)} %get-tuple-element.27, f32[4,4,256]{2,1,0:T(4,128)} %copy-done.14, bf16[256,4,128]{2,0,1:T(8,128)(2,1)} %copy.125, bf16[2048,4,128]{2,0,1:T(8,128)(2,1)} %copy.124), kind=kOutput, calls=%fused_computation.7 | convolution fusion | flops 2458386432 | bytes 60063744 | tf_op jit(solution)/shard_map/tkgd,ukd->kgtu/dot_general | solution.py:43
  120.2 10.3 fusion.22
  130.7 9.8 convolution_multiply_fusion
  140.9 39.5 %all-gather.6.cloned.1.call-done = bf16[8192,2048]{1,0:T(8,128)(2,1)} async-done(((bf16[512,2048]{1,0:T(8,128)(2,1)}), bf16[8192,2048]{1,0:T(8,128)(2,1)}) %all-gather.6.cloned.1.call-update) | async-done | bytes 33554448 | tf_op jit(solution)/shard_map/all_gather | solution.py:110
  180.4 29.0 %fusion.60 = f32[256,8192]{1,0:T(8,128)} fusion(bf16[256,2048]{0,1:T(8,128)(2,1)S(1)} %bitcast.188, bf16[8192,2048]{1,0:T(8,128)(2,1)} %all-gather.6.cloned.1.call-done), kind=kOutput, calls=%fused_computation.101 | convolution fusion | flops 8589934592 | bytes 42991616 | tf_op jit(solution)/shard_map/tc,nc->tn/dot_general | solution.py:107
  209.5 48.0 %all-gather.8.cloned.1.call-done = bf16[8192,512]{1,0:T(8,128)(2,1)} async-done(((bf16[512,512]{1,0:T(8,128)(2,1)}), bf16[8192,512]{1,0:T(8,128)(2,1)}) %all-gather.8.cloned.1.call-update) | async-done | bytes 8388624 | tf_op jit(solution)/shard_map/all_gather | solution.py:116
  257.5 11.4 %convolution_add_fusion.1 = f32[256,8192]{1,0:T(8,128)} fusion(f32[256,8192]{1,0:T(8,128)} %fusion.60, bf16[256,512]{0,1:T(8,128)(2,1)S(1)} %bitcast.185, bf16[8192,512]{1,0:T(8,128)(2,1)} %all-gather.8.cloned.1.call-done), kind=kOutput, calls=%fused_computation.28 | convolution fusion | flops 2149580800 | bytes 25427968 | tf_op jit(solution)/shard_map/tc,nc->tn/dot_general | solution.py:113
  268.9 63.9 %all-gather.10.cloned.1.call-done = bf16[8192,512]{1,0:T(8,128)(2,1)} async-done(((bf16[512,512]{1,0:T(8,128)(2,1)}), bf16[8192,512]{1,0:T(8,128)(2,1)}) %all-gather.10.cloned.1.call-update) | async-done | bytes 8388624 | tf_op jit(solution)/shard_map/all_gather | solution.py:122
  332.8 11.4 %convolution_add_fusion = f32[256,8192]{1,0:T(8,128)} fusion(f32[256,8192]{1,0:T(8,128)} %convolution_add_fusion.1, bf16[256,512]{0,1:T(8,128)(2,1)S(1)} %bitcast.184, bf16[8192,512]{1,0:T(8,128)(2,1)} %all-gather.10.cloned.1.call-done), kind=kOutput, calls=%fused_computation.27 | convolution fusion | flops 2149580800 | bytes 25427968 | tf_op jit(solution)/shard_map/tc,nc->tn/dot_general | solution.py:119
  344.9 4.8 slice.86
  354.3 5.4 copy.148
  359.8 5.5 copy.147
  385.3 8.1 maximum_bitcast_fusion.1
  393.4 17.8 %fusion.59 = (f32[4,4,256]{2,1,0:T(4,128)S(1)}, f32[4,4,256,2304]{2,3,1,0:T(8,128)}) fusion(bf16[256,4,4,128]{0,3,2,1:T(8,128)(2,1)S(1)} %bitcast.187, pred[256,2304]{0,1:T(8,128)(4,1)} %copy-done.11, bf16[256,4,128]{2,0,1:T(8,128)(2,1)} %copy.111, bf16[2048,4,128]{2,0,1:T(8,128)(2,1)} %copy.110), kind=kOutput, calls=%fused_computation.100 | convolution fusion | flops 2458388736 | bytes 41762816 | tf_op jit(solution)/shard_map/sub | solution.py:38
  411.2 30.8 %reduce-scatter.2.cloned.1.call-done = f32[256,4096]{1,0:T(8,128)} async-done(((f32[256,8192]{1,0:T(8,128)}), f32[256,4096]{1,0:T(8,128)}) %reduce-scatter.2.cloned.1.call-update) | async-done | bytes 4194320 | tf_op jit(solution)/shard_map/reduce_scatter | solution.py:126
  445.7 4.9 all-reduce
  450.6 6.9 fusion.29
  457.6 21.8 %fusion.18 = bf16[4,4,256,2304]{2,3,1,0:T(8,128)(2,1)} fusion(f32[4,4,256,2304]{2,3,1,0:T(8,128)} %get-tuple-element.29, f32[4,4,256]{2,1,0:T(4,128)S(1)} %get-tuple-element.28), kind=kLoop, calls=%fused_computation.25 | loop fusion | flops 18874368 | bytes 56639488 | tf_op jit(solution)/shard_map/convert_element_type | solution.py:40
  479.4 132.1 %all-gather.14.cloned.1.call-done = bf16[2048,8192]{1,0:T(8,128)(2,1)} async-done(((bf16[2048,512]{1,0:T(8,128)(2,1)}), bf16[2048,8192]{1,0:T(8,128)(2,1)}) %all-gather.14.cloned.1.call-update) | async-done | bytes 33554448 | tf_op jit(solution)/shard_map/all_gather | solution.py:140
  611.5 58.2 %all-gather.12.cloned.1.call-done = bf16[256,8192]{1,0:T(8,128)(2,1)} async-done(((bf16[256,4096]{1,0:T(8,128)(2,1)}), bf16[256,8192]{1,0:T(8,128)(2,1)}) %all-gather.12.cloned.1.call-update) | async-done | bytes 4194320 | tf_op jit(solution)/shard_map/all_gather | solution.py:135
  669.8 16.7 %convolution_convert_fusion = bf16[256,2048]{1,0:T(8,128)(2,1)} fusion(bf16[256,8192]{1,0:T(8,128)(2,1)} %all-gather.12.cloned.1.call-done, bf16[2048,8192]{1,0:T(8,128)(2,1)} %all-gather.14.cloned.1.call-done), kind=kOutput, calls=%fused_computation.48 | convolution fusion | flops 8590458880 | bytes 38797312 | tf_op jit(solution)/shard_map/td,hd->th/dot_general | solution.py:137
  687.9 10.0 convolution_bitcast_fusion
  700.4 5.4 copy.146
  705.7 9.2 fusion.32
  714.9 18.0 %fusion.25 = f32[2304,4,128]{0,2,1:T(8,128)} fusion(bf16[256,4,4,128]{0,3,2,1:T(8,128)(2,1)} %bitcast.186, bf16[256,4,4,128]{0,3,2,1:T(8,128)(2,1)S(1)} %bitcast.176, f32[4,4,256]{2,1,0:T(4,128)S(1)} %bitcast.193, f32[4,4,256,2304]{2,3,1,0:T(8,128)} %get-tuple-element.29, f32[4,4,256]{2,1,0:T(4,128)S(1)} %get-tuple-element.28, ...), kind=kOutput, calls=%fused_computation.42 | convolution fusion | flops 4875485184 | bytes 46956544 | tf_op jit(solution)/shard_map/kgtu,tkgd->ukd/dot_general | solution.py:49
  737.5 5.4 copy.145
  747.4 9.9 pad_maximum_fusion
  757.4 298.4 %all-reduce.3.cloned.1.call-done = f32[2,2,2048,512]{3,2,1,0:T(8,128)} async-done(((f32[2,2,2048,512]{3,2,1,0:T(8,128)}), f32[2,2,2048,512]{3,2,1,0:T(8,128)}) %all-reduce.3.cloned.1.call-update) | async-done | bytes 16777232 | tf_op jit(solution)/shard_map/psum | solution.py:152
  (89 shorter events, 74.9 us)
Async XLA Ops:
  7.2 4.6 copy-start.12
  7.2 173.2 %all-gather.6.cloned.1.call-start = ((), (), s32[]{:S(2)}) async-start(), calls=%async_computation.1 | async-start | bytes 35651584 | tf_op jit(solution)/shard_map/all_gather | solution.py:110
  7.9 249.6 %all-gather.8.cloned.1.call-start = ((), (), s32[]{:S(2)}) async-start(), calls=%async_computation.2 | async-start | bytes 8912896 | tf_op jit(solution)/shard_map/all_gather | solution.py:116
  8.7 324.2 %all-gather.10.cloned.1.call-start = ((), (), s32[]{:S(2)}) async-start(), calls=%async_computation.3 | async-start | bytes 8912896 | tf_op jit(solution)/shard_map/all_gather | solution.py:122
  9.4 432.6 %reduce-scatter.2.cloned.1.call-start = ((), (), s32[]{:S(2)}) async-start(), calls=%async_computation.4 | async-start | bytes 12582912 | tf_op jit(solution)/shard_map/reduce_scatter | solution.py:126
  12.8 11.2 %copy-start.3 = (bf16[256,4,128]{2,0,1:T(8,128)(2,1)}, bf16[256,4,128]{2,0,1:T(8,128)(2,1)S(1)}, u32[]{:S(2)}) copy-start(bf16[256,4,128]{2,0,1:T(8,128)(2,1)S(1)} %copy.120) | copy-start | bytes 786436
  24.0 19.7 %copy-start.11 = (pred[256,2304]{0,1:T(8,128)(4,1)}, pred[256,2304]{0,1:T(8,128)(4,1)S(1)}, u32[]{:S(2)}) copy-start(pred[256,2304]{0,1:T(8,128)(4,1)S(1)} %fusion.31) | copy-start | bytes 1769476
  43.7 0.6 copy-start.14
  77.9 10.9 %copy-start.2 = (bf16[2048,4,128]{2,0,1:T(8,128)(2,1)S(1)}, bf16[2048,4,128]{2,0,1:T(8,128)(2,1)}, u32[]{:S(2)}) copy-start(bf16[2048,4,128]{2,0,1:T(8,128)(2,1)} %copy.124) | copy-start | bytes 6291460
  78.0 10.9 %copy-start.5 = (bf16[256,4,128]{2,0,1:T(8,128)(2,1)S(1)}, bf16[256,4,128]{2,0,1:T(8,128)(2,1)}, u32[]{:S(2)}) copy-start(bf16[256,4,128]{2,0,1:T(8,128)(2,1)} %copy.125) | copy-start | bytes 786436
  88.5 11.2 %copy-start.1 = (f32[2304,4,128]{0,2,1:T(8,128)}, f32[2304,4,128]{0,2,1:T(8,128)S(1)}, u32[]{:S(2)}) copy-start(f32[2304,4,128]{0,2,1:T(8,128)S(1)} %convolution_bitcast_fusion.1) | copy-start | bytes 14155780
  120.2 10.5 copy-start.4
  130.5 10.0 copy-start
  344.3 267.2 %all-gather.14.cloned.1.call-start = ((), (), s32[]{:S(2)}) async-start(), calls=%async_computation.6 | async-start | bytes 35651584 | tf_op jit(solution)/shard_map/all_gather | solution.py:140
  344.9 324.9 %all-gather.12.cloned.1.call-start = ((), (), s32[]{:S(2)}) async-start(), calls=%async_computation.5 | async-start | bytes 6291456 | tf_op jit(solution)/shard_map/all_gather | solution.py:135
  359.8 5.5 copy-start.15
  359.8 5.5 copy-start.6
  359.8 6.9 copy-start.13
  385.3 8.1 copy-start.7
  457.5 598.2 %all-reduce.3.cloned.1.call-start = ((), (), s32[]{:S(2)}) async-start(), calls=%async_computation.7 | async-start | bytes 33554432 | tf_op jit(solution)/shard_map/psum | solution.py:152
  757.3 298.4 %copy-start.8 = (f32[2,2,128,512]{3,2,1,0:T(8,128)S(1)}, f32[2,2,128,512]{3,2,1,0:T(8,128)}, u32[]{:S(2)}) copy-start(f32[2,2,128,512]{3,2,1,0:T(8,128)} %param.32) | copy-start | bytes 3145732
  757.3 298.4 %copy-start.9 = (f32[2,2,128,512]{3,2,1,0:T(8,128)S(1)}, f32[2,2,128,512]{3,2,1,0:T(8,128)}, u32[]{:S(2)}) copy-start(f32[2,2,128,512]{3,2,1,0:T(8,128)} %param.33) | copy-start | bytes 3145732
  757.3 298.4 %copy-start.10 = (f32[2,2,128,512]{3,2,1,0:T(8,128)S(1)}, f32[2,2,128,512]{3,2,1,0:T(8,128)}, u32[]{:S(2)}) copy-start(f32[2,2,128,512]{3,2,1,0:T(8,128)} %param.34) | copy-start | bytes 3145732
Sparse Core Ops, SparseCore 0:
  9.6 170.7 all-gather.5
  182.6 74.8 all-gather.7
  259.7 73.1 all-gather.9
  344.4 97.4 reduce-scatter.1
  443.4 168.0 all-gather.13
  613.0 56.7 all-gather.11
  757.5 298.2 all-reduce.2
where the time goes:
time: 1080 us; the launch traced here: 1070 us
  waiting for transfers between devices  674 us (62%)
  matrix products  205 us (19%)
  local copies, waits for them, and re-layouts  84.5 us (8%)
  other arithmetic  82.4 us (8%)
  between operations  15.5 us (1%)
    psum x1, waiting for transfers between devices, per_device(): whole_grads = lax.psum(grads, 'dp')  298 us
    all_gather x1, waiting for transfers between devices, per_device(): lax.all_gather(w_output, 'dp', axis=1, tiled=True)  132 us
    all_gather x1, waiting for transfers between devices, per_device(): lax.all_gather(value_weight_above, 'dp', axis=0, tiled=True)  63.9 us
    all_gather x1, waiting for transfers between devices, per_device(): lax.all_gather(grad_local.astype(jnp.bfloat16), 'tensor', axis=1, tiled=T...  58.2 us
    all_gather x1, waiting for transfers between devices, per_device(): lax.all_gather(key_weight_above, 'dp', axis=0, tiled=True)  48 us
    convert_element_type x2, other arithmetic, attend_back(): probs_b = probs.astype(jnp.bfloat16)  43.5 us
    all_gather x1, waiting for transfers between devices, per_device(): lax.all_gather(w_query, 'dp', axis=0, tiled=True)  39.5 us
    sub x2, matrix products, attend_back(): expo = jnp.exp(scores - top)  37.5 us
  transfers between devices with their start and end apart: 7, of which 7 were waited for; matrix products, arithmetic and copies ran while one was open for 25% of the time, Pallas kernels for 0%

commit v1 on v0

--- a/solution.py
+++ b/solution.py
@@ -1,11 +1,16 @@
+import functools
+
 import jax
 import jax.numpy as jnp
 from jax import lax
+from jax.experimental import pallas as pl
+from jax.experimental.pallas import tpu as pltpu
 from jax.sharding import PartitionSpec as P
 
 MODEL_WIDTH = 8192
 HEAD_SIZE = 128
 PREFIX_SLOTS = 2048
+CHUNK = 256
 
 
 norm_eps = 1e-05
@@ -17,43 +22,131 @@
 adam_eps = 1e-08
 
 
-def attend_back(queries, keys, values, out_grad):
-    rows = queries.shape[0]
-    key_rows = keys.shape[0]
-    kv_heads = keys.shape[1] // HEAD_SIZE
-    group = queries.shape[1] // HEAD_SIZE // kv_heads
+def attend_kernel(with_query, query_ref, grad_ref, block_ref, prefix_ref, *rest):
+    if with_query:
+        key_out, value_out, own_key_out, own_value_out, query_out, score_ref, dprob_ref = rest
+    else:
+        key_out, value_out, score_ref, dprob_ref = rest
+    tokens = query_ref.shape[0]
+    slots = prefix_ref.shape[1]
+    step = min(CHUNK, slots)
     scale = HEAD_SIZE ** (-0.5)
-    query_h = queries.reshape(rows, kv_heads, group, HEAD_SIZE)
-    key_h = keys.reshape(key_rows, kv_heads, HEAD_SIZE)
-    value_h = values.reshape(key_rows, kv_heads, HEAD_SIZE)
-    grad_h = out_grad.reshape(rows, kv_heads, group, HEAD_SIZE)
-    scores = (
-        jnp.einsum("tkgd,ukd->kgtu", query_h, key_h, preferred_element_type=jnp.float32) * scale
-    )
-    row_ids = jnp.arange(rows)[:, None]
-    col_ids = jnp.arange(key_rows)[None, :]
-    allowed = (col_ids < PREFIX_SLOTS) | (col_ids - PREFIX_SLOTS <= row_ids)
-    scores = jnp.where(allowed, scores, -jnp.inf)
-    top = jnp.max(scores, axis=-1, keepdims=True)
-    expo = jnp.exp(scores - top)
-    probs = expo / jnp.sum(expo, axis=-1, keepdims=True)
-    probs_b = probs.astype(jnp.bfloat16)
-    attn = jnp.einsum("kgtu,ukd->tkgd", probs_b, value_h, preferred_element_type=jnp.float32)
-    delta = jnp.transpose(jnp.sum(grad_h.astype(jnp.float32) * attn, axis=-1), (1, 2, 0))
-    dprob = jnp.einsum("tkgd,ukd->kgtu", grad_h, value_h, preferred_element_type=jnp.float32)
-    dscore = (probs * (dprob - delta[..., None])).astype(jnp.bfloat16)
-    grad_query = (
-        jnp.einsum("kgtu,ukd->tkgd", dscore, key_h, preferred_element_type=jnp.float32) * scale
-    )
-    grad_key = (
-        jnp.einsum("kgtu,tkgd->ukd", dscore, query_h, preferred_element_type=jnp.float32) * scale
-    )
-    grad_value = jnp.einsum("kgtu,tkgd->ukd", probs_b, grad_h, preferred_element_type=jnp.float32)
-    return (
-        grad_query.reshape(rows, -1),
-        grad_key.reshape(key_rows, -1),
-        grad_value.reshape(key_rows, -1),
-    )
+    spans = [(True, i, step) for i in range(0, slots, step)] + [(False, 0, tokens)]
+    query = query_ref[...]
+    grad = grad_ref[...]
+
+    def rows(which, span):
+        prefix_part, start, size = span
+        ref = prefix_ref if prefix_part else block_ref
+        return ref[which, start : start + size, :]
+
+    def place(span):
+        prefix_part, start, size = span
+        first = start if prefix_part else slots
+        return slice(first, first + size)
+
+    contract_last = (((1,), (1,)), ((), ()))
+    top = jnp.full((1, tokens), -jnp.inf, jnp.float32)
+    for span in spans:
+        score = (
+            lax.dot_general(rows(0, span), query, contract_last, preferred_element_type=jnp.float32)
+            * scale
+        )
+        if not span[0]:
+            key_ids = lax.broadcasted_iota(jnp.int32, score.shape, 0)
+            token_ids = lax.broadcasted_iota(jnp.int32, score.shape, 1)
+            score = jnp.where(key_ids <= token_ids, score, -jnp.inf)
+        score_ref[place(span), :] = score
+        top = jnp.maximum(top, jnp.max(score, axis=0, keepdims=True))
+    total = jnp.zeros((1, tokens), jnp.float32)
+    for span in spans:
+        expo = jnp.exp(score_ref[place(span), :] - top)
+        score_ref[place(span), :] = expo
+        total = total + jnp.sum(expo, axis=0, keepdims=True)
+    inverse = 1.0 / total
+    first_head = pl.program_id(1) == 0
+
+    def add(ref, start, size, value):
+        @pl.when(first_head)
+        def _():
+            ref[start : start + size, :] = value
+
+        @pl.when(jnp.logical_not(first_head))
+        def _():
+            ref[start : start + size, :] += value
+
+    delta = jnp.zeros((1, tokens), jnp.float32)
+    for span in spans:
+        probs = score_ref[place(span), :] * inverse
+        score_ref[place(span), :] = probs
+        probs_b = probs.astype(jnp.bfloat16)
+        dprob = lax.dot_general(
+            rows(1, span), grad, contract_last, preferred_element_type=jnp.float32
+        )
+        dprob_ref[place(span), :] = dprob
+        delta = delta + jnp.sum(probs_b.astype(jnp.float32) * dprob, axis=0, keepdims=True)
+        if span[0] or with_query:
+            ref = value_out if span[0] else own_value_out
+            part = jnp.dot(probs_b, grad, preferred_element_type=jnp.float32)
+            add(ref, span[1], span[2], part)
+    if with_query:
+        grad_query = jnp.zeros((HEAD_SIZE, tokens), jnp.float32)
+    for span in spans:
+        if not (span[0] or with_query):
+            continue
+        dscore = (score_ref[place(span), :] * (dprob_ref[place(span), :] - delta)).astype(
+            jnp.bfloat16
+        )
+        ref = key_out if span[0] else own_key_out
+        part = jnp.dot(dscore, query, preferred_element_type=jnp.float32) * scale
+        add(ref, span[1], span[2], part)
+        if with_query:
+            grad_query = grad_query + lax.dot_general(
+                rows(0, span), dscore, (((0,), (0,)), ((), ())), preferred_element_type=jnp.float32
+            )
+    if with_query:
+        query_out[...] = grad_query.T * scale
+
+
+def layer_back(queries, block_kv, prefix, out_grad, with_query):
+    tokens, width = queries.shape
+    slots, kv_width = prefix.shape[1:]
+    kv_heads = kv_width // HEAD_SIZE
+    group = width // kv_width
+    head_spec = pl.BlockSpec((tokens, HEAD_SIZE), lambda k, g: (0, k * group + g))
+    own_spec = pl.BlockSpec((tokens, HEAD_SIZE), lambda k, g: (0, k))
+    slot_spec = pl.BlockSpec((slots, HEAD_SIZE), lambda k, g: (0, k))
+    f32 = jnp.float32
+    out_shape = [jax.ShapeDtypeStruct((slots, kv_width), f32)] * 2
+    out_specs = [slot_spec] * 2
+    if with_query:
+        out_shape += [jax.ShapeDtypeStruct((tokens, kv_width), f32)] * 2
+        out_shape += [jax.ShapeDtypeStruct((tokens, width), f32)]
+        out_specs += [own_spec] * 2 + [head_spec]
+    matmuls = 5 if with_query else 4
+    keys = slots + tokens
+    return pl.pallas_call(
+        functools.partial(attend_kernel, with_query),
+        grid=(kv_heads, group),
+        in_specs=[
+            head_spec,
+            head_spec,
+            pl.BlockSpec((2, tokens, HEAD_SIZE), lambda k, g: (0, 0, k)),
+            pl.BlockSpec((2, slots, HEAD_SIZE), lambda k, g: (0, 0, k)),
+        ],
+        out_shape=out_shape,
+        out_specs=out_specs,
+        scratch_shapes=[pltpu.VMEM((keys, tokens), f32), pltpu.VMEM((keys, tokens), f32)],
+        compiler_params=pltpu.CompilerParams(
+            dimension_semantics=("arbitrary", "arbitrary"), vmem_limit_bytes=40 * 2**20
+        ),
+        cost_estimate=pl.CostEstimate(
+            flops=2 * matmuls * tokens * keys * width,
+            bytes_accessed=20 * 2**20,
+            transcendentals=tokens * keys * width // HEAD_SIZE,
+        ),
+        name="attend_upper" if with_query else "attend_lower",
+    )(queries, out_grad, block_kv, prefix)
 
 
 def rotate_back(grad, positions):
@@ -70,10 +163,8 @@
     return jnp.concatenate([out_first, out_second], axis=-1).reshape(grad.shape)
 
 
-def layer_back(queries, block_kv, prefix, out_grad):
-    keys = jnp.concatenate([prefix[0], block_kv[0]], axis=0)
-    values = jnp.concatenate([prefix[1], block_kv[1]], axis=0)
-    return attend_back(queries, keys, values, out_grad)
+def share(grads):
+    return [lax.psum_scatter(g, "dp", scatter_dimension=0, tiled=True) for g in grads]
 
 
 def per_device(
@@ -97,13 +188,13 @@
     offsets,
 ):
     tokens = queries_upper.shape[0]
-    grad_query, grad_key, grad_value = layer_back(
-        queries_upper, block_key_value_above, prefix_upper, out_grad_upper
+    upper_key, upper_value, own_key, own_value, grad_query = layer_back(
+        queries_upper, block_key_value_above, prefix_upper, out_grad_upper, True
     )
     positions = (PREFIX_SLOTS + offsets[0] + jnp.arange(tokens)).astype(jnp.float32)
     query_rot = rotate_back(grad_query, positions).astype(jnp.bfloat16)
-    key_rot = rotate_back(grad_key[PREFIX_SLOTS:], positions).astype(jnp.bfloat16)
-    value_rot = grad_value[PREFIX_SLOTS:].astype(jnp.bfloat16)
+    key_rot = rotate_back(own_key, positions).astype(jnp.bfloat16)
+    value_rot = own_value.astype(jnp.bfloat16)
     columns = jnp.einsum(
         "tc,nc->tn",
         query_rot,
@@ -140,19 +231,13 @@
         lax.all_gather(w_output, "dp", axis=1, tiled=True),
         preferred_element_type=jnp.float32,
     ).astype(jnp.bfloat16)
-    lower_query, lower_key, lower_value = layer_back(
-        queries_lower, block_key_value_below, prefix_lower, out_grad_lower
-    )
-    grads = jnp.stack(
-        [
-            jnp.stack([lower_key[:PREFIX_SLOTS], lower_value[:PREFIX_SLOTS]]),
-            jnp.stack([grad_key[:PREFIX_SLOTS], grad_value[:PREFIX_SLOTS]]),
-        ]
-    )
-    whole_grads = lax.psum(grads, "dp")
-    share_rows = PREFIX_SLOTS // lax.axis_size("dp")
-    own_grads = lax.dynamic_slice_in_dim(
-        whole_grads, lax.axis_index("dp") * share_rows, share_rows, 2
+    lower_key, lower_value = layer_back(
+        queries_lower, block_key_value_below, prefix_lower, out_grad_lower, False
+    )
+    upper_key, upper_value = share((upper_key, upper_value))
+    lower_key, lower_value = share((lower_key, lower_value))
+    own_grads = jnp.stack(
+        [jnp.stack([lower_key, lower_value]), jnp.stack([upper_key, upper_value])]
     )
     new_moment_one = beta_one * first_moment_state + (1.0 - beta_one) * own_grads
     new_moment_two = beta_two * second_moment_state + (1.0 - beta_two) * own_grads * own_grads

time: 1080 us -> 985 us (0.912); the launches traced: 1070 us -> 985 us
  Pallas kernels: 0 us -> 169 us
  matrix products: 205 us -> 56.9 us
  local copies, waits for them, and re-layouts: 84.5 us -> 12.7 us
  other arithmetic: 82.4 us -> 19 us
  waiting for transfers between devices: 674 us -> 707 us
    psum x1 -> x0, waiting for transfers between devices: 298 us -> none  [per_device(): whole_grads = lax.psum(grads, 'dp')]
    reduce_scatter x0 -> x4, waiting for transfers between devices: none -> 203 us  [share(): lax.psum_scatter(g, 'dp', scatter_dimension=0, tiled=True)]
    pallas_call x0 -> x2, Pallas kernels: none -> 169 us  [layer_back(): pl.pallas_call(functools.partial(attend_kernel, with_query), grid=(kv_hea...]
    dot_general x8 -> x0, matrix products: 99.1 us -> none  [the longest x2 28.3 us: attend_back(): jnp.einsum('kgtu,tkgd->ukd', dscore, query_h, preferred_element_type=jnp....]
    reduce_scatter x1, waiting for transfers between devices: 30.8 us -> 97 us  [per_device(): lax.psum_scatter(partial_grad, 'tensor', scatter_dimension=1, tiled=True)]
    convert_element_type x2 -> x0, other arithmetic: 43.5 us -> none  [attend_back(): probs_b = probs.astype(jnp.bfloat16)]
    sub x2 -> x0, matrix products: 37.5 us -> none  [attend_back(): expo = jnp.exp(scores - top)]
    all_gather x1, waiting for transfers between devices: 39.5 us -> 67.5 us  [per_device(): lax.all_gather(w_query, 'dp', axis=0, tiled=True)]
  transfers between devices with their start and end apart: 7 -> 10, of which waited for: 7 -> 9; matrix products, arithmetic and copies ran while one was open for 25% -> 6% of each run, Pallas kernels for 0% -> 17%
where the time goes in v1:
time: 985 us
  waiting for transfers between devices  707 us (72%)
  Pallas kernels  169 us (17%)
  matrix products  56.9 us (6%)
  other arithmetic  19 us (2%)
  between operations  15 us (2%)
  local copies, waits for them, and re-layouts  12.7 us (1%)
    reduce_scatter x4, waiting for transfers between devices, share(): lax.psum_scatter(g, 'dp', scatter_dimension=0, tiled=True)  203 us
    pallas_call x2, Pallas kernels, layer_back(): pl.pallas_call(functools.partial(attend_kernel, with_query), grid=(kv_hea...  169 us
    all_gather x1, waiting for transfers between devices, per_device(): lax.all_gather(w_output, 'dp', axis=1, tiled=True)  154 us
    reduce_scatter x1, waiting for transfers between devices, per_device(): lax.psum_scatter(partial_grad, 'tensor', scatter_dimension=1, tiled=True)  97 us
    all_gather x1, waiting for transfers between devices, per_device(): lax.all_gather(w_query, 'dp', axis=0, tiled=True)  67.5 us
    all_gather x1, waiting for transfers between devices, per_device(): lax.all_gather(value_weight_above, 'dp', axis=0, tiled=True)  63.9 us
    all_gather x1, waiting for transfers between devices, per_device(): lax.all_gather(key_weight_above, 'dp', axis=0, tiled=True)  59.1 us
    all_gather x1, waiting for transfers between devices, per_device(): lax.all_gather(grad_local.astype(jnp.bfloat16), 'tensor', axis=1, tiled=T...  58.2 us
  transfers between devices with their start and end apart: 10, of which 9 were waited for; matrix products, arithmetic and copies ran while one was open for 6% of the time, Pallas kernels for 17%

profile of v1, /device:TPU:0, one launch (start us, length us, event | category | flops | bytes accessed | tf_op | source)
XLA Modules:
  0.0 984.6 jit_solution(6807850839384556876)
XLA Ops:
  7.9 0.7 all-gather.8.cloned.1.call-update
  9.4 1.2 copy-done.4
  10.7 1.2 copy-done.5
  11.9 1.0 copy-done.7
  12.9 90.0 %attend_upper.1 = (f32[2048,512]{1,0:T(8,128)S(1)}, f32[2048,512]{1,0:T(8,128)S(1)}, f32[256,512]{1,0:T(8,128)S(1)}, f32[256,512]{1,0:T(8,128)S(1)}, f32[256,2048]{1,0:T(8,128)S(1)}) custom-call(bf16[256,2048]{1,0:T(8,128)(2,1)S(1)} %copy-done.4, bf16[256,2048]{1,0:T(8,128)(2,1)S(1)} %copy-done.5, bf16[2,256,512]{2,1,0:T(8,128)(2,1)S(1)} %copy-done.7, ...), custom_call_target="tpu_custom_call" | custom-call | flops 12079595520 | bytes 20971520 | tf_op jit(solution)/shard_map/attend_upper/pallas_call | solution.py:128
  102.9 1.9 copy-done
  104.9 2.0 copy-done.1
  107.9 1.0 reshape.98
  109.4 1.8 add_convert_fusion.1
  111.5 0.8 add_convert_fusion
  112.9 67.5 %all-gather.6.cloned.1.call-done = bf16[8192,2048]{1,0:T(8,128)(2,1)} async-done(((bf16[512,2048]{1,0:T(8,128)(2,1)}), bf16[8192,2048]{1,0:T(8,128)(2,1)}) %all-gather.6.cloned.1.call-update) | async-done | bytes 33554448 | tf_op jit(solution)/shard_map/all_gather | solution.py:201
  180.4 18.0 %fusion.6 = f32[256,8192]{1,0:T(8,128)} fusion(bf16[8192,2048]{1,0:T(8,128)(2,1)} %all-gather.6.cloned.1.call-done, bf16[32,8,16,128]{3,2,1,0:T(8,128)(2,1)S(1)} %bitcast.27), kind=kOutput, calls=%fused_computation.15 | convolution fusion | flops 8589934592 | bytes 42991616 | tf_op jit(solution)/shard_map/tc,nc->tn/dot_general | solution.py:198
  198.4 59.1 %all-gather.8.cloned.1.call-done = bf16[8192,512]{1,0:T(8,128)(2,1)} async-done(((bf16[512,512]{1,0:T(8,128)(2,1)}), bf16[8192,512]{1,0:T(8,128)(2,1)}) %all-gather.8.cloned.1.call-update) | async-done | bytes 8388624 | tf_op jit(solution)/shard_map/all_gather | solution.py:207
  257.5 11.4 %convolution_add_fusion.1 = f32[256,8192]{1,0:T(8,128)} fusion(f32[256,8192]{1,0:T(8,128)} %fusion.6, bf16[8192,512]{1,0:T(8,128)(2,1)} %all-gather.8.cloned.1.call-done, bf16[32,8,4,128]{3,2,1,0:T(4,128)(2,1)S(1)} %bitcast.26), kind=kOutput, calls=%fused_computation.1 | convolution fusion | flops 2149580800 | bytes 25427968 | tf_op jit(solution)/shard_map/tc,nc->tn/dot_general | solution.py:204
  268.9 63.9 %all-gather.10.cloned.1.call-done = bf16[8192,512]{1,0:T(8,128)(2,1)} async-done(((bf16[512,512]{1,0:T(8,128)(2,1)}), bf16[8192,512]{1,0:T(8,128)(2,1)}) %all-gather.10.cloned.1.call-update) | async-done | bytes 8388624 | tf_op jit(solution)/shard_map/all_gather | solution.py:213
  332.9 11.4 %convolution_add_fusion = f32[256,8192]{1,0:T(8,128)} fusion(f32[256,8192]{1,0:T(8,128)} %convolution_add_fusion.1, bf16[8192,512]{1,0:T(8,128)(2,1)} %all-gather.10.cloned.1.call-done, f32[256,512]{1,0:T(8,128)S(1)} %get-tuple-element.12), kind=kOutput, calls=%fused_computation | convolution fusion | flops 2149711872 | bytes 25690112 | tf_op jit(solution)/shard_map/tc,nc->tn/dot_general | solution.py:210
  344.9 97.0 %reduce-scatter.6.cloned.1.call-done = f32[256,4096]{1,0:T(8,128)} async-done(((f32[256,8192]{1,0:T(8,128)}), f32[256,4096]{1,0:T(8,128)}) %reduce-scatter.6.cloned.1.call-update) | async-done | bytes 4194320 | tf_op jit(solution)/shard_map/reduce_scatter | solution.py:217
  441.9 3.1 fusion
  445.1 4.9 all-reduce
  450.0 6.4 fusion.3
  458.0 153.5 %all-gather.14.cloned.1.call-done = bf16[2048,8192]{1,0:T(8,128)(2,1)} async-done(((bf16[2048,512]{1,0:T(8,128)(2,1)}), bf16[2048,8192]{1,0:T(8,128)(2,1)}) %all-gather.14.cloned.1.call-update) | async-done | bytes 33554448 | tf_op jit(solution)/shard_map/all_gather | solution.py:231
  611.5 58.2 %all-gather.12.cloned.1.call-done = bf16[256,8192]{1,0:T(8,128)(2,1)} async-done(((bf16[256,4096]{1,0:T(8,128)(2,1)}), bf16[256,8192]{1,0:T(8,128)(2,1)}) %all-gather.12.cloned.1.call-update) | async-done | bytes 4194320 | tf_op jit(solution)/shard_map/all_gather | solution.py:226
  669.7 16.1 %convolution_convert_fusion.grad_ref = bf16[256,2048]{1,0:T(8,128)(2,1)S(1)} fusion(bf16[256,8192]{1,0:T(8,128)(2,1)} %all-gather.12.cloned.1.call-done, bf16[2048,8192]{1,0:T(8,128)(2,1)} %all-gather.14.cloned.1.call-done), kind=kOutput, calls=%fused_computation.10 | convolution fusion | flops 8590458880 | bytes 38797312 | tf_op jit(solution)/shard_map/td,hd->th/dot_general | solution.py:228
  685.9 78.7 %attend_lower.1 = (f32[2048,512]{1,0:T(8,128)S(1)}, f32[2048,512]{1,0:T(8,128)S(1)}) custom-call(bf16[256,2048]{1,0:T(8,128)(2,1)S(1)} %copy-done.6, bf16[256,2048]{1,0:T(8,128)(2,1)S(1)} %convolution_convert_fusion.grad_ref, bf16[2,256,512]{2,1,0:T(8,128)(2,1)S(1)} %copy-done.8, bf16[2,2048,512]{2,1,0:T(8,128)(2,1)} %prefix_ref.3), custom_call_target="tpu_custom_call" | custom-call | flops 9663676416 | bytes 20971520 | tf_op jit(solution)/shard_map/attend_lower/pallas_call | solution.py:128
  764.6 1.9 copy-done.2
  766.6 2.0 copy-done.3
  769.3 53.0 %reduce-scatter.12.cloned.1.call-done = f32[128,512]{1,0:T(8,128)} async-done(((f32[2048,512]{1,0:T(8,128)}), f32[128,512]{1,0:T(8,128)}) %reduce-scatter.12.cloned.1.call-update) | async-done | bytes 262160 | tf_op jit(solution)/shard_map/reduce_scatter | solution.py:167
  822.2 1.1 maximum_bitcast_fusion.1
  823.3 74.8 %reduce-scatter.10.cloned.1.call-done = f32[128,512]{1,0:T(8,128)} async-done(((f32[2048,512]{1,0:T(8,128)}), f32[128,512]{1,0:T(8,128)}) %reduce-scatter.10.cloned.1.call-update) | async-done | bytes 262160 | tf_op jit(solution)/shard_map/reduce_scatter | solution.py:167
  898.1 75.2 %reduce-scatter.8.cloned.1.call-done = f32[128,512]{1,0:T(8,128)} async-done(((f32[2048,512]{1,0:T(8,128)}), f32[128,512]{1,0:T(8,128)}) %reduce-scatter.8.cloned.1.call-update) | async-done | bytes 262160 | tf_op jit(solution)/shard_map/reduce_scatter | solution.py:167
  973.3 1.1 maximum_bitcast_fusion
  974.4 3.4 divide_subtract_fusion
  (47 shorter events, 6.2 us)
Async XLA Ops:
  7.2 173.2 %all-gather.6.cloned.1.call-start = ((), (), s32[]{:S(2)}) async-start(), calls=%async_computation.5 | async-start | bytes 35651584 | tf_op jit(solution)/shard_map/all_gather | solution.py:201
  7.9 249.6 %all-gather.8.cloned.1.call-start = ((), (), s32[]{:S(2)}) async-start(), calls=%async_computation.6 | async-start | bytes 8912896 | tf_op jit(solution)/shard_map/all_gather | solution.py:207
  8.6 324.2 %all-gather.10.cloned.1.call-start = ((), (), s32[]{:S(2)}) async-start(), calls=%async_computation.7 | async-start | bytes 8912896 | tf_op jit(solution)/shard_map/all_gather | solution.py:213
  9.4 432.6 %reduce-scatter.6.cloned.1.call-start = ((), (), s32[]{:S(2)}) async-start(), calls=%async_computation.8 | async-start | bytes 12582912 | tf_op jit(solution)/shard_map/reduce_scatter | solution.py:217
  9.4 1.2 copy-start.4
  10.7 1.2 copy-start.5
  11.9 1.0 copy-start.7
  102.9 1.9 copy-start
  104.9 2.0 copy-start.1
  344.2 0.7 copy-start.12
  344.2 97.7 %copy-start.9 = (bf16[256,4096]{1,0:T(8,128)(2,1)S(1)}, bf16[256,4096]{1,0:T(8,128)(2,1)}, u32[]{:S(2)}) copy-start(bf16[256,4096]{1,0:T(8,128)(2,1)} %param.18) | copy-start | bytes 6291460
  344.3 267.2 %all-gather.14.cloned.1.call-start = ((), (), s32[]{:S(2)}) async-start(), calls=%async_computation.10 | async-start | bytes 35651584 | tf_op jit(solution)/shard_map/all_gather | solution.py:231
  344.9 324.9 %all-gather.12.cloned.1.call-start = ((), (), s32[]{:S(2)}) async-start(), calls=%async_computation.9 | async-start | bytes 6291456 | tf_op jit(solution)/shard_map/all_gather | solution.py:226
  456.4 312.9 %reduce-scatter.14.cloned.1.call-start = ((), (), s32[]{:S(2)}) async-start(), calls=%async_computation.14 | async-start | bytes 4456448 | tf_op jit(solution)/shard_map/reduce_scatter | solution.py:167
  457.1 365.1 %reduce-scatter.12.cloned.1.call-start = ((), (), s32[]{:S(2)}) async-start(), calls=%async_computation.13 | async-start | bytes 4456448 | tf_op jit(solution)/shard_map/reduce_scatter | solution.py:167
  457.9 228.0 %copy-start.6 = (bf16[256,2048]{1,0:T(8,128)(2,1)S(1)}, bf16[256,2048]{1,0:T(8,128)(2,1)}, u32[]{:S(2)}) copy-start(bf16[256,2048]{1,0:T(8,128)(2,1)} %query_ref.3) | copy-start | bytes 3145732
  457.9 228.0 %copy-start.8 = (bf16[2,256,512]{2,1,0:T(8,128)(2,1)S(1)}, bf16[2,256,512]{2,1,0:T(8,128)(2,1)}, u32[]{:S(2)}) copy-start(bf16[2,256,512]{2,1,0:T(8,128)(2,1)} %block_ref.3) | copy-start | bytes 1572868
  457.9 440.2 %reduce-scatter.10.cloned.1.call-start = ((), (), s32[]{:S(2)}) async-start(), calls=%async_computation.12 | async-start | bytes 4456448 | tf_op jit(solution)/shard_map/reduce_scatter | solution.py:167
  764.6 2.0 copy-start.2
  766.6 2.0 copy-start.3
  768.6 205.8 %copy-start.10 = (f32[2,2,128,512]{3,2,1,0:T(8,128)S(1)}, f32[2,2,128,512]{3,2,1,0:T(8,128)}, u32[]{:S(2)}) copy-start(f32[2,2,128,512]{3,2,1,0:T(8,128)} %param.32) | copy-start | bytes 3145732
  768.6 205.8 %copy-start.11 = (f32[2,2,128,512]{3,2,1,0:T(8,128)S(1)}, f32[2,2,128,512]{3,2,1,0:T(8,128)}, u32[]{:S(2)}) copy-start(f32[2,2,128,512]{3,2,1,0:T(8,128)} %param.33) | copy-start | bytes 3145732
  768.6 204.7 %reduce-scatter.8.cloned.1.call-start = ((), (), s32[]{:S(2)}) async-start(), calls=%async_computation.11 | async-start | bytes 4456448 | tf_op jit(solution)/shard_map/reduce_scatter | solution.py:167
Sparse Core Ops, SparseCore 0:
  9.6 170.7 all-gather.5
  182.6 74.8 all-gather.7
  259.7 73.1 all-gather.9
  344.4 97.4 reduce-scatter.5
  443.4 168.0 all-gather.13
  613.0 56.7 all-gather.11
  674.1 72.7 reduce-scatter.13
  750.8 71.4 reduce-scatter.11
  826.6 71.4 reduce-scatter.9
  901.8 71.4 reduce-scatter.7

commit v2 on v1

--- a/solution.py
+++ b/solution.py
@@ -164,7 +164,36 @@
 
 
 def share(grads):
-    return [lax.psum_scatter(g, "dp", scatter_dimension=0, tiled=True) for g in grads]
+    both = jnp.concatenate(grads, axis=1)
+    mine = lax.psum_scatter(both, "dp", scatter_dimension=0, tiled=True)
+    return jnp.split(mine, len(grads), axis=1)
+
+
+def exchange_sum(values, axis):
+    size, me = lax.axis_size(axis), lax.axis_index(axis)
+    width = values.shape[1] // size
+
+    def part(owner):
+        return lax.dynamic_slice_in_dim(values, owner * width, width, 1)
+
+    total = part(me)
+    for step in range(1, size):
+        pairs = [(i, (i + step) % size) for i in range(size)]
+        total = total + lax.ppermute(part((me + step) % size), axis, pairs)
+    return total
+
+
+def exchange_whole(part, axis):
+    size, me = lax.axis_size(axis), lax.axis_index(axis)
+    width = part.shape[1]
+    whole = jnp.zeros((part.shape[0], width * size), part.dtype)
+    whole = lax.dynamic_update_slice_in_dim(whole, part, me * width, 1)
+    for step in range(1, size):
+        pairs = [(i, (i + step) % size) for i in range(size)]
+        owner = (me - step + size) % size
+        got = lax.ppermute(part, axis, pairs)
+        whole = lax.dynamic_update_slice_in_dim(whole, got, owner * width, 1)
+    return whole
 
 
 def per_device(
@@ -195,26 +224,14 @@
     query_rot = rotate_back(grad_query, positions).astype(jnp.bfloat16)
     key_rot = rotate_back(own_key, positions).astype(jnp.bfloat16)
     value_rot = own_value.astype(jnp.bfloat16)
-    columns = jnp.einsum(
+    weights = jnp.concatenate([w_query, key_weight_above, value_weight_above], axis=1)
+    partial_grad = jnp.einsum(
         "tc,nc->tn",
-        query_rot,
-        lax.all_gather(w_query, "dp", axis=0, tiled=True),
+        jnp.concatenate([query_rot, key_rot, value_rot], axis=1),
+        lax.all_gather(weights, "dp", axis=0, tiled=True),
         preferred_element_type=jnp.float32,
     )
-    columns = columns + jnp.einsum(
-        "tc,nc->tn",
-        key_rot,
-        lax.all_gather(key_weight_above, "dp", axis=0, tiled=True),
-        preferred_element_type=jnp.float32,
-    )
-    columns = columns + jnp.einsum(
-        "tc,nc->tn",
-        value_rot,
-        lax.all_gather(value_weight_above, "dp", axis=0, tiled=True),
-        preferred_element_type=jnp.float32,
-    )
-    partial_grad = columns
-    hidden_grad = lax.psum_scatter(partial_grad, "tensor", scatter_dimension=1, tiled=True)
+    hidden_grad = exchange_sum(partial_grad, "tensor")
     hidden_f = x_hidden.astype(jnp.float32)
     gained = norm_gain.astype(jnp.float32) * hidden_grad
     square_sum, cross_sum = lax.psum(
@@ -223,7 +240,7 @@
     recip = 1.0 / jnp.sqrt(square_sum[:, None] / MODEL_WIDTH + norm_eps)
     cross = cross_sum[:, None] / MODEL_WIDTH
     grad_local = resid_grad.astype(jnp.float32) + recip * gained - hidden_f * recip**3 * cross
-    grad_hidden = lax.all_gather(grad_local.astype(jnp.bfloat16), "tensor", axis=1, tiled=True)
+    grad_hidden = exchange_whole(grad_local.astype(jnp.bfloat16), "tensor")
     columns = grad_hidden
     out_grad_lower = jnp.einsum(
         "td,hd->th",

time: 985 us -> 667 us (0.68)
  waiting for transfers between devices: 707 us -> 388 us
  matrix products: 56.9 us -> 41.7 us
    reduce_scatter x5 -> x2, waiting for transfers between devices: 300 us -> 104 us  [share(): mine = lax.psum_scatter(both, 'dp', scatter_dimension=0, tiled=True)]
    all_gather x1, waiting for transfers between devices: 154 us -> 0.01 us  [per_device(): lax.all_gather(w_output, 'dp', axis=1, tiled=True)]
    ppermute x0 -> x2, waiting for transfers between devices: none -> 137 us  [the longest x1 91.7 us: exchange_sum(): total = total + lax.ppermute(part((me + step) % size), axis, pairs)]
    all_gather x4 -> x1, waiting for transfers between devices: 249 us -> 146 us  [per_device(): lax.all_gather(weights, 'dp', axis=0, tiled=True)]
    dot_general x3 -> x1, matrix products: 40.8 us -> 24.1 us  [per_device(): jnp.einsum('tc,nc->tn', jnp.concatenate([query_rot, key_rot, value_rot],...]
    concatenate x0 -> x3, other arithmetic: none -> 12.2 us  [the longest x2 8.97 us: share(): both = jnp.concatenate(grads, axis=1)]
  transfers between devices with their start and end apart: 10 -> 6, of which waited for: 9 -> 4; matrix products, arithmetic and copies ran while one was open for 6% -> 11% of each run, Pallas kernels for 17% -> 25%
where the time goes in v2:
time: 667 us; the launch traced here: 666 us
  waiting for transfers between devices  388 us (58%)
  Pallas kernels  169 us (25%)
  matrix products  41.7 us (6%)
  other arithmetic  28.8 us (4%)
  local copies, waits for them, and re-layouts  16.2 us (2%)
  between operations  14.6 us (2%)
    pallas_call x2, Pallas kernels, layer_back(): pl.pallas_call(functools.partial(attend_kernel, with_query), grid=(kv_hea...  169 us
    all_gather x1, waiting for transfers between devices, per_device(): lax.all_gather(weights, 'dp', axis=0, tiled=True)  146 us
    reduce_scatter x2, waiting for transfers between devices, share(): mine = lax.psum_scatter(both, 'dp', scatter_dimension=0, tiled=True)  104 us
    ppermute x1, waiting for transfers between devices, exchange_sum(): total = total + lax.ppermute(part((me + step) % size), axis, pairs)  91.7 us
    ppermute x1, waiting for transfers between devices, exchange_whole(): got = lax.ppermute(part, axis, pairs)  45.1 us
    dot_general x1, matrix products, per_device(): jnp.einsum('tc,nc->tn', jnp.concatenate([query_rot, key_rot, value_rot],...  24.1 us
    dot_general x1, matrix products, per_device(): jnp.einsum('td,hd->th', columns, lax.all_gather(w_output, 'dp', axis=1, t...  17.6 us
  transfers between devices with their start and end apart: 6, of which 4 were waited for; matrix products, arithmetic and copies ran while one was open for 11% of the time, Pallas kernels for 25%

profile of v2, /device:TPU:0, one launch (start us, length us, event | category | flops | bytes accessed | tf_op | source)
XLA Modules:
  0.0 666.4 jit_solution(7458057409575143108)
XLA Ops:
  7.2 3.2 pad_maximum_fusion.2
  10.5 0.7 all-gather.5.cloned.1.call-update
  11.4 1.2 copy-done.2
  12.7 1.2 copy-done.3
  13.9 90.0 %attend_upper.1 = (f32[2048,512]{1,0:T(8,128)S(1)}, f32[2048,512]{1,0:T(8,128)S(1)}, f32[256,512]{1,0:T(8,128)S(1)}, f32[256,512]{1,0:T(8,128)S(1)}, f32[256,2048]{1,0:T(8,128)S(1)}) custom-call(bf16[256,2048]{1,0:T(8,128)(2,1)S(1)} %copy-done.2, bf16[256,2048]{1,0:T(8,128)(2,1)S(1)} %copy-done.3, bf16[2,256,512]{2,1,0:T(8,128)(2,1)S(1)} %copy-done.5, ...), custom_call_target="tpu_custom_call" | custom-call | flops 12079595520 | bytes 20971520 | tf_op jit(solution)/shard_map/attend_upper/pallas_call | solution.py:128
  103.9 0.8 copy-done
  104.7 4.5 pad_maximum_fusion.1
  109.4 0.8 copy-done.1
  111.1 0.5 multiply_cosine_fusion
  111.6 0.5 add_convert_fusion.1
  112.5 0.4 copy.21
  112.9 0.8 add_convert_fusion
  113.7 0.6 pad_maximum_fusion.3
  114.6 145.8 %all-gather.3.cloned.1.call-done = bf16[8192,3072]{1,0:T(8,128)(2,1)} async-done(((bf16[512,3072]{1,0:T(8,128)(2,1)}), bf16[8192,3072]{1,0:T(8,128)(2,1)}) %all-gather.3.cloned.1.call-update) | async-done | bytes 50331664 | tf_op jit(solution)/shard_map/all_gather | solution.py:231
  260.4 24.1 %fusion.5 = f32[256,8192]{1,0:T(8,128)} fusion(bf16[8192,3072]{1,0:T(8,128)(2,1)} %all-gather.3.cloned.1.call-done, bf16[256,512]{1,0:T(8,128)(2,1)S(1)} %convert_element_type.48, bf16[256,512]{1,0:T(8,128)(2,1)S(1)} %bitcast.31, bf16[256,2048]{1,0:T(8,128)(2,1)S(1)} %bitcast.30), kind=kOutput, calls=%fused_computation.15 | convolution fusion | flops 12889620480 | bytes 60293120 | tf_op jit(solution)/shard_map/tc,nc->tn/dot_general | solution.py:228
  284.5 4.8 constant_dynamic-slice_fusion
  289.4 1.6 collective-permute-start
  290.9 91.7 %collective-permute-done = f32[256,4096]{1,0:T(8,128)} collective-permute-done((f32[256,4096]{1,0:T(8,128)}, f32[256,4096]{1,0:T(8,128)}, u32[]{:S(2)}, u32[]{:S(2)}) %collective-permute-start) | collective-permute-done | bytes 4194336 | tf_op jit(solution)/shard_map/ppermute | solution.py:182
  382.6 4.9 fusion
  387.5 5.2 all-reduce
  392.6 2.5 broadcast_in_dim.2
  395.1 5.6 constant_dynamic-update-slice_fusion.1
  400.7 1.6 collective-permute-start.1
  402.3 45.1 %collective-permute-done.1 = bf16[256,4096]{1,0:T(8,128)(2,1)S(1)} collective-permute-done((bf16[256,4096]{1,0:T(8,128)(2,1)S(1)}, bf16[256,4096]{1,0:T(8,128)(2,1)S(1)}, u32[]{:S(2)}, u32[]{:S(2)}) %collective-permute-start.1) | collective-permute-done | bytes 2097184 | tf_op jit(solution)/shard_map/ppermute | solution.py:194
  447.3 1.5 constant_dynamic-update-slice_fusion
  448.8 17.6 %convolution_convert_fusion.grad_ref = bf16[256,2048]{1,0:T(8,128)(2,1)S(1)} fusion(bf16[256,8192]{1,0:T(8,128)(2,1)} %constant_dynamic-update-slice_fusion, bf16[2048,8192]{1,0:T(8,128)(2,1)} %all-gather.5.cloned.1.call-done), kind=kOutput, calls=%fused_computation.12 | convolution fusion | flops 8590458880 | bytes 38797312 | tf_op jit(solution)/shard_map/td,hd->th/dot_general | solution.py:245
  466.5 78.7 %attend_lower.1 = (f32[2048,512]{1,0:T(8,128)S(1)}, f32[2048,512]{1,0:T(8,128)S(1)}) custom-call(bf16[256,2048]{1,0:T(8,128)(2,1)S(1)} %copy-done.4, bf16[256,2048]{1,0:T(8,128)(2,1)S(1)} %convolution_convert_fusion.grad_ref, bf16[2,256,512]{2,1,0:T(8,128)(2,1)S(1)} %copy-done.6, bf16[2,2048,512]{2,1,0:T(8,128)(2,1)} %prefix_ref.3), custom_call_target="tpu_custom_call" | custom-call | flops 9663676416 | bytes 20971520 | tf_op jit(solution)/shard_map/attend_lower/pallas_call | solution.py:128
  545.2 4.5 pad_maximum_fusion
  549.7 1.2 slice_bitcast_fusion.1
  551.0 104.4 %reduce-scatter.3.cloned.1.call-done = f32[128,1024]{1,0:T(8,128)} async-done(((f32[2048,1024]{1,0:T(8,128)}), f32[128,1024]{1,0:T(8,128)}) %reduce-scatter.3.cloned.1.call-update) | async-done | bytes 524304 | tf_op jit(solution)/shard_map/reduce_scatter | solution.py:168
  655.3 1.1 slice_bitcast_fusion.3
  656.5 3.4 divide_subtract_fusion
  (40 shorter events, 1.7 us)
Async XLA Ops:
  7.2 253.2 %all-gather.3.cloned.1.call-start = ((), (), s32[]{:S(2)}) async-start(), calls=%async_computation.2 | async-start | bytes 53477376 | tf_op jit(solution)/shard_map/all_gather | solution.py:231
  10.4 1.0 copy-start.5
  10.4 438.4 %all-gather.5.cloned.1.call-start = ((), (), s32[]{:S(2)}) async-start(), calls=%async_computation.3 | async-start | bytes 35651584 | tf_op jit(solution)/shard_map/all_gather | solution.py:248
  11.2 538.6 %reduce-scatter.5.cloned.1.call-start = ((), (), s32[]{:S(2)}) async-start(), calls=%async_computation.5 | async-start | bytes 8912896 | tf_op jit(solution)/shard_map/reduce_scatter | solution.py:168
  11.4 1.2 copy-start.2
  12.7 1.2 copy-start.3
  103.9 0.8 copy-start
  109.2 1.1 copy-start.1
  109.2 546.2 %reduce-scatter.3.cloned.1.call-start = ((), (), s32[]{:S(2)}) async-start(), calls=%async_computation.4 | async-start | bytes 8912896 | tf_op jit(solution)/shard_map/reduce_scatter | solution.py:168
  284.5 6.4 copy-start.11
  284.5 98.1 %copy-start.7 = (bf16[256,4096]{1,0:T(8,128)(2,1)S(1)}, bf16[256,4096]{1,0:T(8,128)(2,1)}, u32[]{:S(2)}) copy-start(bf16[256,4096]{1,0:T(8,128)(2,1)} %param.18) | copy-start | bytes 6291460
  289.4 93.3 %collective-permute-start = (f32[256,4096]{1,0:T(8,128)}, f32[256,4096]{1,0:T(8,128)}, u32[]{:S(2)}, u32[]{:S(2)}) collective-permute-start(f32[256,4096]{1,0:T(8,128)} %constant_dynamic-slice_fusion), channel_id=1, source_target_pairs={{0,1},{1,0},{2,3},{3,2},{4,5},{5,4},{6,7},{7,6},{8,9},{9,8},{10,11... | collective-permute-start | bytes 12582920 | tf_op jit(solution)/shard_map/ppermute | solution.py:182
  392.6 2.5 copy-start.8
  400.7 46.6 %collective-permute-start.1 = (bf16[256,4096]{1,0:T(8,128)(2,1)S(1)}, bf16[256,4096]{1,0:T(8,128)(2,1)S(1)}, u32[]{:S(2)}, u32[]{:S(2)}) collective-permute-start(bf16[256,4096]{1,0:T(8,128)(2,1)S(1)} %get-tuple-element.25), channel_id=1, source_target_pairs={{0,1},{1,0},{2,3},{3,2},{4,5},{5,4},{6,7},{7,6},{8,9},{9,8},{10,11... | collective-permute-start | bytes 6291464 | tf_op jit(solution)/shard_map/ppermute | solution.py:194
  448.8 17.6 %copy-start.4 = (bf16[256,2048]{1,0:T(8,128)(2,1)S(1)}, bf16[256,2048]{1,0:T(8,128)(2,1)}, u32[]{:S(2)}) copy-start(bf16[256,2048]{1,0:T(8,128)(2,1)} %query_ref.3) | copy-start | bytes 3145732
  448.8 17.6 %copy-start.6 = (bf16[2,256,512]{2,1,0:T(8,128)(2,1)S(1)}, bf16[2,256,512]{2,1,0:T(8,128)(2,1)}, u32[]{:S(2)}) copy-start(bf16[2,256,512]{2,1,0:T(8,128)(2,1)} %block_ref.3) | copy-start | bytes 1572868
  549.7 106.8 %copy-start.9 = (f32[2,2,128,512]{3,2,1,0:T(8,128)S(1)}, f32[2,2,128,512]{3,2,1,0:T(8,128)}, u32[]{:S(2)}) copy-start(f32[2,2,128,512]{3,2,1,0:T(8,128)} %param.32) | copy-start | bytes 3145732
  549.7 106.8 %copy-start.10 = (f32[2,2,128,512]{3,2,1,0:T(8,128)S(1)}, f32[2,2,128,512]{3,2,1,0:T(8,128)}, u32[]{:S(2)}) copy-start(f32[2,2,128,512]{3,2,1,0:T(8,128)} %param.33) | copy-start | bytes 3145732
Sparse Core Ops, SparseCore 0:
  10.5 249.8 all-gather.2
  262.0 168.0 all-gather.4
  434.1 104.5 reduce-scatter.4
  549.8 105.4 reduce-scatter.2
